TPU v7x, 32 devices: a whole 2x2x4 slice. The times are simulated.
32 devices in a mesh: grp: 2 (over y), gx: 8 (over z, x), gy: 2 (over core).
Axes of the slice: x: 2, y: 2, z: 4, core: 2. Of those that a mesh axis runs over, the one named last changes fastest.
Arguments:
- block: float32 [64, 8, 96, 256], P(None, None, ('grp', 'gx'), 'gy'), parts along dimension 2, may hold values from -6 to 6
- hop: float32 [98, 8, 8], P('grp'), parts along dimension 0, may hold values from -0.3125 to 0.3125
- onsite: float32 [8, 96, 256], P(None, ('grp', 'gx'), 'gy'), parts along dimension 1, may hold values from -1 to 1
- offsets: int32 [49, 2], replicated, may hold values from -3 to 3, as said below
Outputs:
- basis: float32 [64, 8, 96, 256], P(None, None, ('grp', 'gx'), 'gy'), parts along dimension 2
There are 2 independent parts, one for each index of `grp`. A program takes and returns all parts, laid end to end along the dimension named above; an argument that names none is the same for every part. Nothing has to cross between parts.
Inputs may be any that keep to these rules, and one draw needn't show every extreme that they name: `offsets`: each pair (dx, dy) with both entries in -3 .. 3 stands in exactly one row.
All inputs are finite; a program needn't handle non-finite values.
Results may differ from a plain program's by a relative error of at most 0.0001.
Values sent between devices are 32-bit elements; how exact they have to be, the bound alone decides.
A program may use at most 64 MiB of HBM per device.

v0:
```python
import jax
import jax.numpy as jnp
from jax import lax
from jax.sharding import PartitionSpec as P

ORB = 8
REACH = 3
DEGREE = 4
NB = 49


shift_centre = 1.25
half_width = 2.25


def padded_2(array, sides, width):
    for axis, dim in sides:
        peers, length = (lax.axis_size(axis), array.shape[dim])
        up = [(i, (i + 1) % peers) for i in range(peers)]
        down = [(j, i) for i, j in up]
        last = lax.slice_in_dim(array, length - width, length, axis=dim)
        first = lax.slice_in_dim(array, 0, width, axis=dim)
        before = lax.ppermute(last, axis, up)
        after = lax.ppermute(first, axis, down)
        array = jnp.concatenate([before, array, after], axis=dim)
    return array


def build_stencil(hop, offsets):
    side = 2 * REACH + 1
    position = (offsets[:, 0] + REACH) * side + (offsets[:, 1] + REACH)
    slots = jnp.arange(NB, dtype=jnp.int32)
    onehot = (position[:, None] == slots[None, :]).astype(jnp.float32)
    flat = jnp.dot(
        onehot.T,
        hop.reshape(NB, ORB * ORB),
        precision=lax.Precision.HIGHEST,
        preferred_element_type=jnp.float32,
    )
    raw = jnp.transpose(flat.reshape(side, side, ORB, ORB), (2, 3, 0, 1))
    mirror = jnp.transpose(raw, (1, 0, 2, 3))[:, :, ::-1, ::-1]
    return 0.5 * (raw + mirror)


def hopping(padded, stencil):
    return lax.conv_general_dilated(
        padded,
        stencil,
        (1, 1),
        "VALID",
        dimension_numbers=("NCHW", "OIHW", "NCHW"),
        precision=lax.Precision.HIGHEST,
        preferred_element_type=jnp.float32,
    )


def extend(field, width):
    return padded_2(field, (("gx", 2), ("gy", 3)), width)


def advance(hopped, current, energies, previous):
    return (
        2.0 * (hopped + energies[None] * current - shift_centre * current) / half_width - previous
    )


def per_device(block, hop, onsite, offsets):
    stencil = build_stencil(hop, offsets)
    vectors = block.shape[0]
    first_hop = hopping(extend(block, REACH), stencil)
    current = (first_hop + onsite[None] * block - shift_centre * block) / half_width
    previous = block
    for step in range(DEGREE - 1):
        following = advance(hopping(extend(current, REACH), stencil), current, onsite, previous)
        previous, current = (current, following)
    local_rows = current.shape[1] * current.shape[2] * current.shape[3]
    flat = current.reshape(vectors, local_rows)
    local_gram = jnp.dot(
        flat, flat.T, precision=lax.Precision.HIGHEST, preferred_element_type=jnp.float32
    )
    total_rows = local_rows * lax.axis_size("gx") * lax.axis_size("gy")
    gram = lax.psum(local_gram, ("gx", "gy")) / total_rows
    lower = jnp.linalg.cholesky(gram)
    inverse = lax.linalg.triangular_solve(
        lower, jnp.eye(vectors, dtype=jnp.float32), left_side=True, lower=True
    )
    basis = jnp.dot(
        inverse, flat, precision=lax.Precision.HIGHEST, preferred_element_type=jnp.float32
    )
    return basis.reshape(current.shape)


def solution(mesh):
    return jax.shard_map(
        per_device,
        mesh=mesh,
        in_specs=(
            P(None, None, ("grp", "gx"), "gy"),
            P("grp", None, None),
            P(None, ("grp", "gx"), "gy"),
            P(),
        ),
        out_specs=P(None, None, ("grp", "gx"), "gy"),
        check_vma=False,
    )
```

profile of v0, /device:TPU:0, one launch (start us, length us, event | category | flops | bytes accessed | tf_op | source)
XLA Modules:
  0.0 548.5 jit_solution(9051879785537565130)
XLA Ops:
  0.0 2.6 fusion.71
  2.6 6.0 %collective-permute-start.1 = (f32[64,8,3,128]{3,1,2,0:T(8,128)}, f32[64,8,3,128]{3,1,2,0:T(8,128)}, u32[]{:S(2)}, u32[]{:S(2)}) collective-permute-start(f32[64,8,3,128]{3,1,2,0:T(8,128)} %get-tuple-element.20), channel_id=1, source_target_pairs={{2,0},{4,2},{6,4},{8,6},{10,8},{12,10},{14,12},{0,14},{3,1},{5,3},... | collective-permute-start | bytes 2359304 | tf_op jit(solution)/shard_map/ppermute | solution.py:24
  8.6 2.3 copy.76
  11.4 1.2 copy.79
  12.6 27.6 %collective-permute-done.1 = f32[64,8,3,128]{3,1,2,0:T(8,128)} collective-permute-done((f32[64,8,3,128]{3,1,2,0:T(8,128)}, f32[64,8,3,128]{3,1,2,0:T(8,128)}, u32[]{:S(2)}, u32[]{:S(2)}) %collective-permute-start.1) | collective-permute-done | bytes 786464 | tf_op jit(solution)/shard_map/ppermute | solution.py:24
  40.3 2.8 copy.77
  43.0 2.8 copy.75
  45.8 1.5 pad_maximum_fusion.11
  48.6 0.9 copy.80
  50.2 64.8 %fusion.42 = (f32[64,8,6,128]{0,1,3,2:T(8,128)S(1)}, f32[64,8,6,128]{0,1,3,2:T(8,128)}) fusion(f32[64,8,6,128]{0,1,3,2:T(8,128)} %copy-done.5, f32[8,6,128]{0,2,1:T(8,128)} %copy.80, f32[8,8,7,7]{1,0,3,2:T(8,128)} %fusion.54, f32[64,8,12,3]{0,1,3,2:T(8,128)} %copy-done.16, f32[64,8,3,128]{0,1,3,2:T(8,128)} %copy.77, f32[64,8,3,128]{0,1,3,2:T(8,128)} %copy.75, ...), kind=kOutput, calls=%fused_computation.46 | convolution fusion | flops 1854947328 | bytes 6476032 | tf_op jit(solution)/shard_map/conv_general_dilated | solution.py:46
  115.0 1.9 fusion.70
  116.9 2.8 copy.84
  119.7 2.8 collective-permute-start.5
  122.5 2.8 copy.83
  125.5 30.8 %collective-permute-done.5 = f32[64,8,3,128]{3,1,2,0:T(8,128)} collective-permute-done((f32[64,8,3,128]{3,1,2,0:T(8,128)}, f32[64,8,3,128]{3,1,2,0:T(8,128)}, u32[]{:S(2)}, u32[]{:S(2)}) %collective-permute-start.5) | collective-permute-done | bytes 786464 | tf_op jit(solution)/shard_map/ppermute | solution.py:24
  156.3 2.8 copy.86
  159.1 2.8 copy.85
  161.8 1.5 pad_maximum_fusion.8
  163.9 1.0 copy.87
  165.3 63.6 %multiply_subtract_fusion.2 = f32[64,8,6,128]{0,1,3,2:T(8,128)S(1)} fusion(f32[64,8,6,128]{0,1,3,2:T(8,128)} %copy-done.5, f32[64,8,6,128]{0,1,3,2:T(8,128)} %get-tuple-element.22, f32[8,8,7,7]{1,0,3,2:T(8,128)S(1)} %copy-done.14, f32[64,8,12,3]{0,1,3,2:T(8,128)} %collective-permute-done.7, f32[64,8,3,128]{0,1,3,2:T(8,128)} %copy.86, ...), kind=kOutput, calls=%fused_computation.44 | convolution fusion | flops 1856913408 | bytes 8073472 | tf_op jit(solution)/shard_map/conv_general_dilated | solution.py:46
  228.9 2.1 fusion.69
  231.6 2.8 copy.90
  234.3 2.8 collective-permute-start.9
  237.2 2.8 copy.89
  239.9 31.2 %collective-permute-done.9 = f32[64,8,3,128]{3,1,2,0:T(8,128)} collective-permute-done((f32[64,8,3,128]{3,1,2,0:T(8,128)}, f32[64,8,3,128]{3,1,2,0:T(8,128)}, u32[]{:S(2)}, u32[]{:S(2)}) %collective-permute-start.9) | collective-permute-done | bytes 786464 | tf_op jit(solution)/shard_map/ppermute | solution.py:24
  271.1 2.8 copy.92
  273.8 2.8 copy.91
  276.6 1.1 pad_maximum_fusion.5
  279.6 63.7 %multiply_subtract_fusion.1 = f32[64,8,6,128]{0,1,3,2:T(8,128)S(1)} fusion(f32[64,8,6,128]{0,1,3,2:T(8,128)S(1)} %get-tuple-element.21, f32[64,8,6,128]{0,1,3,2:T(8,128)S(1)} %copy-done.3, f32[8,8,7,7]{1,0,3,2:T(8,128)S(1)} %copy-done.14, f32[64,8,12,3]{0,1,3,2:T(8,128)S(1)} %collective-permute-done.11, f32[64,8,3,128]{0,1,3,2:T(8,128)S(1)} %copy-done.10, ...), kind=kOutput, calls=%fused_computation.43 | convolution fusion | flops 1855340544 | bytes 6476032 | tf_op jit(solution)/shard_map/conv_general_dilated | solution.py:46
  343.3 1.5 fusion.68
  345.5 1.4 copy.94
  346.9 2.8 collective-permute-start.13
  349.7 2.9 copy.93
  352.8 30.9 %collective-permute-done.13 = f32[64,8,3,128]{3,1,2,0:T(8,128)} collective-permute-done((f32[64,8,3,128]{3,1,2,0:T(8,128)}, f32[64,8,3,128]{3,1,2,0:T(8,128)}, u32[]{:S(2)}, u32[]{:S(2)}) %collective-permute-start.13) | collective-permute-done | bytes 786464 | tf_op jit(solution)/shard_map/ppermute | solution.py:24
  383.7 2.8 copy.96
  386.4 2.8 copy.95
  389.2 1.0 pad_maximum_fusion.2
  392.1 63.5 %multiply_subtract_fusion = f32[64,8,6,128]{0,1,3,2:T(8,128)S(1)} fusion(f32[64,8,6,128]{0,1,3,2:T(8,128)S(1)} %copy-done.4, f32[64,8,6,128]{0,1,3,2:T(8,128)S(1)} %copy-done.7, f32[8,8,7,7]{1,0,3,2:T(8,128)S(1)} %copy-done.14, f32[64,8,12,3]{0,1,3,2:T(8,128)S(1)} %collective-permute-done.15, f32[64,8,3,128]{0,1,3,2:T(8,128)S(1)} %copy-done.9, ...), kind=kOutput, calls=%fused_computation.42 | convolution fusion | flops 1855340544 | bytes 6476032 | tf_op jit(solution)/shard_map/conv_general_dilated | solution.py:46
  455.6 1.6 copy-done.8
  457.2 6.0 %fusion.51 = f32[64,64]{0,1:T(8,128)S(1)} fusion(f32[64,8,6,128]{0,1,3,2:T(8,128)S(1)} %multiply_subtract_fusion), kind=kOutput, calls=%fused_computation.49 | convolution fusion | flops 301989888 | bytes 1589248 | tf_op jit(solution)/shard_map/dot_general | solution.py:78
  463.2 4.0 copy.101
  467.2 60.4 %psum.7 = f32[64,64]{0,1:T(8,128)S(1)} all-reduce(f32[64,64]{0,1:T(8,128)S(1)} %fusion.51), channel_id=1, replica_groups=mesh['grp'=2,'gx'=8,'gy'=2] {'gx','gy'}, use_global_device_ids=true, to_apply=%region_0.0 | all-reduce | flops 4096 | bytes 32768 | tf_op jit(solution)/shard_map/psum | solution.py:82
  527.7 5.8 %cholesky.17 = f32[64,64]{1,0:T(8,128)S(1)} custom-call(f32[64,64]{1,0:T(8,128)S(1)} %fusion.59), custom_call_target="Cholesky" | custom-call | tf_op jit(solution)/shard_map/jit(cholesky)/cholesky | solution.py:83
  534.9 4.9 custom-call.6
  540.0 1.6 reshape.39
  541.6 2.1 dot_general.22
  543.7 2.3 fusion.49
  546.0 2.1 copy.103
  (71 shorter events, 10.3 us)
Async XLA Ops:
  0.0 11.0 %copy-start = (f32[49,8,8]{0,2,1:T(8,128)S(1)}, f32[49,8,8]{0,2,1:T(8,128)}, u32[]{:S(2)}) copy-start(f32[49,8,8]{0,2,1:T(8,128)} %param.5) | copy-start | bytes 37636
  2.6 8.3 %copy-start.17 = (s32[49,2]{0,1:T(2,128)S(1)}, s32[49,2]{0,1:T(2,128)}, u32[]{:S(2)}) copy-start(s32[49,2]{0,1:T(2,128)} %param.7) | copy-start | bytes 1180
  2.6 37.6 %collective-permute-start.1 = (f32[64,8,3,128]{3,1,2,0:T(8,128)}, f32[64,8,3,128]{3,1,2,0:T(8,128)}, u32[]{:S(2)}, u32[]{:S(2)}) collective-permute-start(f32[64,8,3,128]{3,1,2,0:T(8,128)} %get-tuple-element.20), channel_id=1, source_target_pairs={{2,0},{4,2},{6,4},{8,6},{10,8},{12,10},{14,12},{0,14},{3,1},{5,3},... | collective-permute-start | bytes 2359304 | tf_op jit(solution)/shard_map/ppermute | solution.py:24
  8.6 34.4 %collective-permute-start = (f32[64,8,3,128]{3,1,2,0:T(8,128)}, f32[64,8,3,128]{3,1,2,0:T(8,128)}, u32[]{:S(2)}, u32[]{:S(2)}) collective-permute-start(f32[64,8,3,128]{3,1,2,0:T(8,128)} %get-tuple-element.19), channel_id=1, source_target_pairs={{0,2},{2,4},{4,6},{6,8},{8,10},{10,12},{12,14},{14,0},{1,3},{3,5},... | collective-permute-start | bytes 2359304 | tf_op jit(solution)/shard_map/ppermute | solution.py:23
  10.9 36.4 %copy-start.5 = (f32[64,8,6,128]{0,1,3,2:T(8,128)}, f32[64,8,6,128]{0,1,3,2:T(8,128)S(1)}, u32[]{:S(2)}) copy-start(f32[64,8,6,128]{0,1,3,2:T(8,128)S(1)} %copy.76) | copy-start | bytes 4718596
  45.8 2.1 copy-start.13
  45.8 2.8 copy-start.15
  47.3 2.2 collective-permute-start.3
  47.3 2.8 collective-permute-start.2
  49.5 0.7 copy-start.16
  119.7 36.6 %collective-permute-start.5 = (f32[64,8,3,128]{3,1,2,0:T(8,128)}, f32[64,8,3,128]{3,1,2,0:T(8,128)}, u32[]{:S(2)}, u32[]{:S(2)}) collective-permute-start(f32[64,8,3,128]{3,1,2,0:T(8,128)} %copy.84), channel_id=1, source_target_pairs={{2,0},{4,2},{6,4},{8,6},{10,8},{12,10},{14,12},{0,14},{3,1},{5,3},... | collective-permute-start | bytes 2359304 | tf_op jit(solution)/shard_map/ppermute | solution.py:24
  125.3 33.8 %collective-permute-start.4 = (f32[64,8,3,128]{3,1,2,0:T(8,128)}, f32[64,8,3,128]{3,1,2,0:T(8,128)}, u32[]{:S(2)}, u32[]{:S(2)}) collective-permute-start(f32[64,8,3,128]{3,1,2,0:T(8,128)} %copy.83), channel_id=1, source_target_pairs={{0,2},{2,4},{4,6},{6,8},{8,10},{10,12},{12,14},{14,0},{1,3},{3,5},... | collective-permute-start | bytes 2359304 | tf_op jit(solution)/shard_map/ppermute | solution.py:23
  161.8 3.4 copy-start.14
  163.4 1.9 collective-permute-start.7
  163.4 1.9 collective-permute-start.6
  228.9 2.7 copy-start.2
  234.3 36.8 %collective-permute-start.9 = (f32[64,8,3,128]{3,1,2,0:T(8,128)}, f32[64,8,3,128]{3,1,2,0:T(8,128)}, u32[]{:S(2)}, u32[]{:S(2)}) collective-permute-start(f32[64,8,3,128]{3,1,2,0:T(8,128)} %copy.90), channel_id=1, source_target_pairs={{2,0},{4,2},{6,4},{8,6},{10,8},{12,10},{14,12},{0,14},{3,1},{5,3},... | collective-permute-start | bytes 2359304 | tf_op jit(solution)/shard_map/ppermute | solution.py:24
  239.9 33.9 %collective-permute-start.8 = (f32[64,8,3,128]{3,1,2,0:T(8,128)}, f32[64,8,3,128]{3,1,2,0:T(8,128)}, u32[]{:S(2)}, u32[]{:S(2)}) collective-permute-start(f32[64,8,3,128]{3,1,2,0:T(8,128)} %copy.89), channel_id=1, source_target_pairs={{0,2},{2,4},{4,6},{6,8},{8,10},{10,12},{12,14},{14,0},{1,3},{3,5},... | collective-permute-start | bytes 2359304 | tf_op jit(solution)/shard_map/ppermute | solution.py:23
  276.6 2.8 copy-start.3
  276.6 2.8 copy-start.10
  276.6 3.0 copy-start.12
  277.8 1.4 collective-permute-start.11
  277.8 1.6 collective-permute-start.10
  343.3 2.2 copy-start.6
  346.9 36.8 %collective-permute-start.13 = (f32[64,8,3,128]{3,1,2,0:T(8,128)}, f32[64,8,3,128]{3,1,2,0:T(8,128)}, u32[]{:S(2)}, u32[]{:S(2)}) collective-permute-start(f32[64,8,3,128]{3,1,2,0:T(8,128)} %copy.94), channel_id=1, source_target_pairs={{2,0},{4,2},{6,4},{8,6},{10,8},{12,10},{14,12},{0,14},{3,1},{5,3},... | collective-permute-start | bytes 2359304 | tf_op jit(solution)/shard_map/ppermute | solution.py:24
  349.7 39.5 %copy-start.7 = (f32[64,8,6,128]{0,1,3,2:T(8,128)S(1)}, f32[64,8,6,128]{0,1,3,2:T(8,128)}, u32[]{:S(2)}) copy-start(f32[64,8,6,128]{0,1,3,2:T(8,128)} %copy-done.6) | copy-start | bytes 4718596
  352.7 33.8 %collective-permute-start.12 = (f32[64,8,3,128]{3,1,2,0:T(8,128)}, f32[64,8,3,128]{3,1,2,0:T(8,128)}, u32[]{:S(2)}, u32[]{:S(2)}) collective-permute-start(f32[64,8,3,128]{3,1,2,0:T(8,128)} %copy.93), channel_id=1, source_target_pairs={{0,2},{2,4},{4,6},{6,8},{8,10},{10,12},{12,14},{14,0},{1,3},{3,5},... | collective-permute-start | bytes 2359304 | tf_op jit(solution)/shard_map/ppermute | solution.py:23
  389.2 2.7 copy-start.4
  389.2 2.7 copy-start.9
  389.2 2.9 copy-start.11
  390.2 1.4 collective-permute-start.15
  390.3 1.6 collective-permute-start.14
  455.6 1.6 copy-start.8
  541.6 6.5 %copy-start.1 = (f32[49,8,8]{0,2,1:T(8,128)S(1)}, f32[49,8,8]{0,2,1:T(8,128)}, u32[]{:S(2)}) copy-start(f32[49,8,8]{0,2,1:T(8,128)} %param.5) | copy-start | bytes 37636
where the time goes:
time: 557 us; the launch traced here: 548 us
  matrix products  265 us (48%)
  waiting for transfers between devices  123 us (22%)
  local copies, waits for them, and re-layouts  64.8 us (12%)
  blocking collectives  60.4 us (11%)
  other arithmetic  18.1 us (3%)
  starting transfers between devices  17 us (3%)
    conv_general_dilated x4, matrix products, hopping(): lax.conv_general_dilated(padded, stencil, (1, 1), 'VALID', dimension_numb...  256 us
    ppermute x8, waiting for transfers between devices, padded_2(): after = lax.ppermute(first, axis, down)  123 us
    psum x1, blocking collectives, per_device(): gram = lax.psum(local_gram, ('gx', 'gy')) / total_rows  60.4 us
    slice x7, local copies, waits for them, and re-layouts, padded_2(): last = lax.slice_in_dim(array, length - width, length, axis=dim)  16.5 us
    ppermute x8, starting transfers between devices, padded_2(): after = lax.ppermute(first, axis, down)  14.6 us
  transfers between devices with their start and end apart: 16, of which 9 were waited for; matrix products, arithmetic and copies ran while one was open for 5% of the time, Pallas kernels for 0%

commit v1 on v0

--- a/solution.py
+++ b/solution.py
@@ -1,6 +1,10 @@
+import functools
+
 import jax
 import jax.numpy as jnp
 from jax import lax
+from jax.experimental import pallas as pl
+from jax.experimental.pallas import tpu as pltpu
 from jax.sharding import PartitionSpec as P
 
 ORB = 8
@@ -64,7 +68,7 @@
     )
 
 
-def per_device(block, hop, onsite, offsets):
+def per_device_halo(block, hop, onsite, offsets):
     stencil = build_stencil(hop, offsets)
     vectors = block.shape[0]
     first_hop = hopping(extend(block, REACH), stencil)
@@ -90,6 +94,340 @@
     return basis.reshape(current.shape)
 
 
+LANES = 128
+TY = 16
+MESH = pl.DeviceIdType.MESH
+
+
+def split_bf16(value):
+    high = value.astype(jnp.bfloat16)
+    low = (value - high.astype(jnp.float32)).astype(jnp.bfloat16)
+    return high, low
+
+
+def band_weights(stencil):
+    side = 2 * REACH + 1
+    t = jnp.transpose(stencil, (2, 3, 1, 0)).reshape(side * side * ORB, ORB)
+    lane = jnp.arange(LANES)
+    spread = (lane[None, :] // TY == jnp.arange(ORB)[:, None]).astype(jnp.float32)
+    wide = jnp.dot(t, spread, precision=lax.Precision.HIGHEST, preferred_element_type=jnp.float32)
+    wide = wide.reshape(side, side, 1, ORB, 1, LANES)
+    yy = jnp.arange(TY)
+    rel = jnp.stack([yy, jnp.where(yy < TY // 2, yy + TY, yy - TY)])
+    dy = rel[:, :, None] - (lane % TY)[None, None, :]
+    total = jnp.zeros((side, 2, ORB, TY, LANES), jnp.float32)
+    for k in range(side):
+        total = total + jnp.where((dy == k - REACH)[None, :, None], wide[:, k], 0.0)
+    band = total.reshape(side, 2 * LANES, LANES)
+    zero = jnp.zeros((1, 2 * LANES, LANES), jnp.float32)
+    full = jnp.concatenate(
+        [jnp.concatenate([band, zero], axis=0), jnp.concatenate([zero, band], axis=0)], axis=2
+    )
+    high = lax.reduce_precision(full, 8, 7)
+    return high.astype(jnp.bfloat16), (full - high).astype(jnp.bfloat16)
+
+
+def swap_blocks(value):
+    row = lax.broadcasted_iota(jnp.int32, value.shape, 1)
+    blk = lax.broadcasted_iota(jnp.int32, value.shape, 2) // TY
+    for bit in (1, 2, 4):
+        a = (row // bit) % 2
+        b = (blk // bit) % 2
+        up = pltpu.roll(pltpu.roll(value, 8 - bit, 1), TY * bit, 2)
+        down = up if bit == 4 else pltpu.roll(pltpu.roll(value, bit, 1), LANES - TY * bit, 2)
+        value = jnp.where(a == b, value, jnp.where(a < b, up, down))
+    return value
+
+
+def filter_kernel(
+    sizes, block_ref, onsite_ref, wh_ref, wl_ref, out_ref, gram_ref,
+    recv, energies, state, sh, sl, back, gathered, grams,
+    send_sems, recv_sems, local_sems, back_send, back_recv, back_local, gram_send, gram_recv,
+):
+    ngx, ngy, chunks, lx = sizes
+    peers = ngx * ngy
+    nx = ngx * lx
+    half = nx // 2
+    piece = lx * ORB
+    gx, gy = lax.axis_index("gx"), lax.axis_index("gy")
+    me = gx * ngy + gy
+
+    def peer(k):
+        other = lax.rem(me + k, peers)
+        return other, {"gx": other // ngy, "gy": lax.rem(other, ngy)}
+
+    barrier = pltpu.get_barrier_semaphore()
+
+    def greet(k, carry):
+        pl.semaphore_signal(barrier, inc=1, device_id=peer(k)[1], device_id_type=MESH)
+        return carry
+
+    lax.fori_loop(1, peers, greet, 0)
+    pl.semaphore_wait(barrier, peers - 1)
+
+    def rows_of(vector):
+        return pl.ds(vector * piece, piece)
+
+    def landing(c):
+        return recv.at[c, gy, pl.ds(gx * piece, piece)]
+
+    def send_onsite(k, carry):
+        pltpu.make_async_remote_copy(
+            src_ref=onsite_ref, dst_ref=landing(chunks), send_sem=send_sems.at[chunks],
+            recv_sem=recv_sems.at[chunks], device_id=peer(k)[1], device_id_type=MESH,
+        ).start()
+        return carry
+
+    pltpu.make_async_copy(onsite_ref, landing(chunks), local_sems.at[chunks]).start()
+    lax.fori_loop(1, peers, send_onsite, 0)
+
+    def send_chunk(c, carry):
+        pltpu.make_async_copy(
+            block_ref.at[rows_of(c * peers + me)], landing(c), local_sems.at[c]
+        ).start()
+
+        def one(k, carry):
+            other, where = peer(k)
+            pltpu.make_async_remote_copy(
+                src_ref=block_ref.at[rows_of(c * peers + other)], dst_ref=landing(c),
+                send_sem=send_sems.at[c], recv_sem=recv_sems.at[c],
+                device_id=where, device_id_type=MESH,
+            ).start()
+            return carry
+
+        return lax.fori_loop(1, peers, one, carry)
+
+    lax.fori_loop(0, chunks, send_chunk, 0)
+
+    others = (peers - 1) * piece
+
+    def wait_chunk(c):
+        pltpu.make_async_copy(
+            block_ref.at[pl.ds(0, others)], gathered.at[pl.ds(0, others)], recv_sems.at[c]
+        ).wait()
+        pltpu.make_async_copy(block_ref.at[pl.ds(0, piece)], landing(c), local_sems.at[c]).wait()
+
+    def unpack(c, store):
+        for g in range(ngy):
+            for q in range(0, nx, 8):
+                tile = recv[c, g, pl.ds(q * ORB, 8 * ORB)].reshape(8, ORB, LANES)
+                tile = swap_blocks(tile)
+                for i in range(8):
+                    x = q + i
+                    store(x % 2, x // 2, g, tile[i])
+
+    wait_chunk(chunks)
+
+    def store_energy(xr, r, g, tile):
+        energies[xr, r, pl.ds(g * 8, 8), :] = tile - shift_centre
+
+    unpack(chunks, store_energy)
+
+    lane = lax.broadcasted_iota(jnp.int32, (1, TY, LANES), 2)
+    near = lax.rem(lane, TY) < TY // 2
+    low_rows = {1: (1, [(0, half - 1), (half + 1, 0), (half + 2, 1)]),
+                0: (2, [(0, half - 2), (1, half - 1), (half + 2, 0)])}
+
+    def one_chunk(c, carry):
+        wait_chunk(c)
+
+        def store_state(xr, r, g, tile):
+            state[0, xr, r, pl.ds(g * 8, 8), :] = tile
+            state[1, xr, r, pl.ds(g * 8, 8), :] = jnp.zeros_like(tile)
+
+        unpack(c, store_state)
+
+        def step(k, carry):
+            now = lax.rem(k, 2)
+            for xr in range(2):
+                par = 1 - xr
+                start, wraps = low_rows[par]
+                for r in range(0, half, 4):
+                    v = state[now, xr, pl.ds(r, 4)]
+                    edge = jnp.where(near, pltpu.roll(v, TY - 1, 1), pltpu.roll(v, 1, 1))
+                    both = jnp.concatenate([v, edge], axis=2)
+                    high, low = split_bf16(both)
+                    sh[par, pl.ds(start + r, 4)] = high
+                    sl[par, pl.ds(start + r, 4)] = low
+                for to, r in wraps:
+                    sh[par, to] = sh[par, start + r]
+                    sl[par, to] = sl[par, start + r]
+            alpha = jnp.where(k == 0, 1.0 / half_width, 2.0 / half_width)
+            for r in range(0, half, 8):
+                acc = jnp.zeros((8 * TY, 2 * LANES), jnp.float32)
+                for j in range(2 * REACH + 2):
+                    rows = pl.ds(r + j // 2, 8)
+                    vh = sh[j % 2, rows].reshape(8 * TY, 2 * LANES)
+                    vl = sl[j % 2, rows].reshape(8 * TY, 2 * LANES)
+                    acc += jnp.dot(vh, wh_ref[j], preferred_element_type=jnp.float32)
+                    acc += jnp.dot(vl, wh_ref[j], preferred_element_type=jnp.float32)
+                    acc += jnp.dot(vh, wl_ref[j], preferred_element_type=jnp.float32)
+                for xr in range(2):
+                    hopped = acc[:, xr * LANES:(xr + 1) * LANES].reshape(8, TY, LANES)
+                    v = state[now, xr, pl.ds(r, 8)]
+                    e = energies[xr, pl.ds(r, 8)]
+                    old = state[1 - now, xr, pl.ds(r, 8)]
+                    state[1 - now, xr, pl.ds(r, 8)] = alpha * (hopped + e * v) - old
+            return carry
+
+        lax.fori_loop(0, DEGREE, step, 0)
+
+        for g in range(ngy):
+            for q in range(0, nx, 8):
+                tile = jnp.stack(
+                    [state[DEGREE % 2, (q + i) % 2, (q + i) // 2, pl.ds(g * 8, 8), :] for i in range(8)]
+                )
+                back[c, g, pl.ds(q * ORB, 8 * ORB)] = swap_blocks(tile).reshape(8 * ORB, LANES)
+
+        home = rows_of(c * peers + me)
+        pltpu.make_async_copy(
+            back.at[c, gy, pl.ds(gx * piece, piece)], gathered.at[home], back_local.at[c]
+        ).start()
+
+        def one(k, carry):
+            other, where = peer(k)
+            pltpu.make_async_remote_copy(
+                src_ref=back.at[c, lax.rem(other, ngy), pl.ds((other // ngy) * piece, piece)],
+                dst_ref=gathered.at[home], send_sem=back_send.at[c], recv_sem=back_recv.at[c],
+                device_id=where, device_id_type=MESH,
+            ).start()
+            return carry
+
+        return lax.fori_loop(1, peers, one, carry)
+
+    lax.fori_loop(0, chunks, one_chunk, 0)
+
+    def wait_back(c, carry):
+        pltpu.make_async_copy(
+            block_ref.at[pl.ds(0, others)], gathered.at[pl.ds(0, others)], back_recv.at[c]
+        ).wait()
+        pltpu.make_async_copy(
+            block_ref.at[pl.ds(0, piece)], gathered.at[pl.ds(0, piece)], back_local.at[c]
+        ).wait()
+        return carry
+
+    lax.fori_loop(0, chunks, wait_back, 0)
+
+    nvec = chunks * peers
+    total = jnp.zeros((2 * nvec, nvec), jnp.float32)
+
+    def gram_step(q, total):
+        a = gathered[pl.ds(2 * q, nvec, stride=piece), :]
+        b = gathered[pl.ds(2 * q + 1, nvec, stride=piece), :]
+        high, low = split_bf16(jnp.concatenate([a, b], axis=1))
+        return total + lax.dot_general(
+            jnp.concatenate([high, low], axis=0), high, (((1,), (1,)), ((), ())),
+            preferred_element_type=jnp.float32,
+        )
+
+    total = lax.fori_loop(0, piece // 2, gram_step, total)
+    cross = total[nvec:]
+    local = total[:nvec] + cross + cross.T
+    grams[me] = jnp.concatenate([local[: nvec // 2], local[nvec // 2:]], axis=1)
+
+    def send_gram(k, carry):
+        pltpu.make_async_remote_copy(
+            src_ref=grams.at[me], dst_ref=grams.at[me], send_sem=gram_send,
+            recv_sem=gram_recv, device_id=peer(k)[1], device_id_type=MESH,
+        ).start()
+        return carry
+
+    lax.fori_loop(1, peers, send_gram, 0)
+    out_copy = pltpu.make_async_copy(gathered, out_ref, local_sems.at[chunks])
+    out_copy.start()
+    pltpu.make_async_copy(
+        grams.at[pl.ds(0, peers - 1)], grams.at[pl.ds(0, peers - 1)], gram_recv
+    ).wait()
+    total = grams[0]
+    for d in range(1, peers):
+        total = total + grams[d]
+    gram_ref[...] = total
+
+    def drain(c, carry):
+        pltpu.make_async_copy(
+            block_ref.at[pl.ds(0, others)], gathered.at[pl.ds(0, others)], send_sems.at[c]
+        ).wait()
+        return carry
+
+    lax.fori_loop(0, chunks + 1, drain, 0)
+
+    def drain_back(c, carry):
+        pltpu.make_async_copy(
+            block_ref.at[pl.ds(0, others)], gathered.at[pl.ds(0, others)], back_send.at[c]
+        ).wait()
+        return carry
+
+    lax.fori_loop(0, chunks, drain_back, 0)
+    pltpu.make_async_copy(
+        grams.at[pl.ds(0, peers - 1)], grams.at[pl.ds(0, peers - 1)], gram_send
+    ).wait()
+    out_copy.wait()
+
+
+def per_device_whole(block, hop, onsite, offsets):
+    ngx, ngy = lax.axis_size("gx"), lax.axis_size("gy")
+    peers = ngx * ngy
+    nvec, _, lx, ly = block.shape
+    chunks = nvec // peers
+    nx = ngx * lx
+    piece = lx * ORB
+    wh, wl = band_weights(build_stencil(hop, offsets))
+    rows = jnp.transpose(block, (0, 2, 1, 3)).reshape(nvec * piece, ly)
+    energy_rows = jnp.transpose(onsite, (1, 0, 2)).reshape(piece, ly)
+    vmem = pl.BlockSpec(memory_space=pltpu.VMEM)
+    hbm = pl.BlockSpec(memory_space=pl.ANY)
+    filtered, packed = pl.pallas_call(
+        functools.partial(filter_kernel, (ngx, ngy, chunks, lx)),
+        out_shape=(
+            jax.ShapeDtypeStruct((nvec * piece, ly), jnp.float32),
+            jax.ShapeDtypeStruct((nvec // 2, LANES), jnp.float32),
+        ),
+        in_specs=[vmem, vmem, vmem, vmem],
+        out_specs=(hbm, vmem),
+        scratch_shapes=[
+            pltpu.VMEM((chunks + 1, ngy, nx * ORB, LANES), jnp.float32),
+            pltpu.VMEM((2, nx // 2, TY, LANES), jnp.float32),
+            pltpu.VMEM((2, 2, nx // 2, TY, LANES), jnp.float32),
+            pltpu.VMEM((2, nx // 2 + REACH, TY, 2 * LANES), jnp.bfloat16),
+            pltpu.VMEM((2, nx // 2 + REACH, TY, 2 * LANES), jnp.bfloat16),
+            pltpu.VMEM((chunks, ngy, nx * ORB, LANES), jnp.float32),
+            pltpu.VMEM((nvec * piece, LANES), jnp.float32),
+            pltpu.VMEM((peers, nvec // 2, LANES), jnp.float32),
+            pltpu.SemaphoreType.DMA((chunks + 1,)),
+            pltpu.SemaphoreType.DMA((chunks + 1,)),
+            pltpu.SemaphoreType.DMA((chunks + 1,)),
+            pltpu.SemaphoreType.DMA((chunks,)),
+            pltpu.SemaphoreType.DMA((chunks,)),
+            pltpu.SemaphoreType.DMA((chunks,)),
+            pltpu.SemaphoreType.DMA,
+            pltpu.SemaphoreType.DMA,
+        ],
+        compiler_params=pltpu.CompilerParams(
+            collective_id=0, has_side_effects=True, vmem_limit_bytes=48 * 1024 * 1024
+        ),
+    )(rows, energy_rows, wh, wl)
+    gram = jnp.concatenate([packed[:, :nvec], packed[:, nvec:]], axis=0)
+    gram = gram / (piece * ly * peers)
+    lower = jnp.linalg.cholesky(gram)
+    inverse = lax.linalg.triangular_solve(
+        lower, jnp.eye(nvec, dtype=jnp.float32), left_side=True, lower=True
+    )
+    return jnp.einsum(
+        "mn,nxoy->moxy", inverse, filtered.reshape(nvec, lx, ORB, ly),
+        precision=lax.Precision.HIGHEST, preferred_element_type=jnp.float32,
+    )
+
+
+def per_device(block, hop, onsite, offsets):
+    ngx, ngy = lax.axis_size("gx"), lax.axis_size("gy")
+    nvec, orbitals, lx, ly = block.shape
+    fits = (
+        nvec % (ngx * ngy) == 0 and nvec == 64 and orbitals == ORB and ly == LANES
+        and ngy == 2 and (ngx * lx) % 16 == 0
+    )
+    return (per_device_whole if fits else per_device_halo)(block, hop, onsite, offsets)
+
+
 def solution(mesh):
     return jax.shard_map(
         per_device,

time: 557 us -> 114 us (0.20); the launches traced: 548 us -> 114 us
  matrix products: 265 us -> 2.96 us
  waiting for transfers between devices: 123 us -> 0 us
  Pallas kernels: 0 us -> 92.9 us
  local copies, waits for them, and re-layouts: 64.8 us -> 3.6 us
  blocking collectives: 60.4 us -> 0 us
  starting transfers between devices: 17 us -> 0 us
    conv_general_dilated x4 -> x0, matrix products: 256 us -> none  [hopping(): lax.conv_general_dilated(padded, stencil, (1, 1), 'VALID', dimension_numb...]
    ppermute x16 -> x0, waiting for transfers between devices: 123 us -> none  [the longest x8 123 us: padded_2(): after = lax.ppermute(first, axis, down)]
    pallas_call x0 -> x1, Pallas kernels: none -> 92.9 us  [per_device_whole(): pl.pallas_call(functools.partial(filter_kernel, (ngx, ngy, chunks, lx)),...]
    psum x1 -> x0, blocking collectives: 60.4 us -> none  [per_device(): gram = lax.psum(local_gram, ('gx', 'gy')) / total_rows]
    slice x10 -> x1, local copies, waits for them, and re-layouts: 23.5 us -> 0.01 us  [per_device_whole(): gram = jnp.concatenate([packed[:, :nvec], packed[:, nvec:]], axis=0)]
    ppermute x8 -> x0, local copies, waits for them, and re-layouts: 22 us -> none  [the longest x4 11 us: padded_2(): before = lax.ppermute(last, axis, up)]
    ppermute x16 -> x0, starting transfers between devices: 17 us -> none  [the longest x8 14.6 us: padded_2(): after = lax.ppermute(first, axis, down)]
    unnamed x38 -> x6, local copies, waits for them, and re-layouts: 7.28 us -> 1.04 us
  transfers between devices with their start and end apart: 16 -> 0, of which waited for: 9 -> 0; matrix products, arithmetic and copies ran while one was open for 5% -> 0% of each run, Pallas kernels for 0% -> 0%
where the time goes in v1:
time: 114 us
  Pallas kernels  92.9 us (81%)
  other arithmetic  14 us (12%)
  local copies, waits for them, and re-layouts  3.6 us (3%)
  matrix products  2.96 us (3%)
    pallas_call x1, Pallas kernels, per_device_whole(): pl.pallas_call(functools.partial(filter_kernel, (ngx, ngy, chunks, lx)),...  92.9 us
    another operation x3, other arithmetic, per_device_whole(): lower = jnp.linalg.cholesky(gram)  6.52 us
    another operation x2, other arithmetic, per_device_whole(): lax.linalg.triangular_solve(lower, jnp.eye(nvec, dtype=jnp.float32), left...  5.55 us

profile of v1, /device:TPU:0, one launch (start us, length us, event | category | flops | bytes accessed | tf_op | source)
XLA Modules:
  0.0 113.7 jit_solution(5351977890970289577)
XLA Ops:
  0.0 0.0 copy-start
  0.0 0.8 add_bitcast_fusion
  0.8 0.1 subtract_compare_fusion.6
  1.0 0.0 copy-done
  1.1 0.4 fusion.16
  1.5 0.1 rev.3
  1.6 0.1 copy.5
  1.8 0.3 convolution_bitcast_fusion
  2.1 0.5 fusion.6
  2.6 0.0 copy-start.1
  2.6 0.0 copy-start.2
  2.6 0.3 fusion
  3.0 1.0 copy-done.1
  4.0 0.0 copy-done.2
  4.0 92.9 %shard_map.46 = (f32[3072,128]{1,0:T(8,128)S(1)}, f32[32,128]{1,0:T(8,128)S(1)}) custom-call(f32[3072,128]{1,0:T(8,128)S(1)} %bitcast.114, f32[48,128]{1,0:T(8,128)S(1)} %bitcast.116, bf16[8,256,256]{2,1,0:T(8,128)(2,1)S(1)} %get-tuple-element.10.wh_ref, bf16[8,256,256]{2,1,0:T(8,128)(2,1)S(1)} %get-tuple-element.9.wl_ref), custom_call_target="tpu_custom_call" | custom-call | tf_op jit(solution)/shard_map/pallas_call | solution.py:379
  96.9 0.1 copy.7
  97.0 0.1 maximum_multiply_fusion
  97.1 0.1 copy.9
  97.2 0.1 fusion.19
  97.3 5.8 %cholesky.17 = f32[64,64]{1,0:T(8,128)S(1)} custom-call(f32[64,64]{1,0:T(8,128)S(1)} %fusion.19), custom_call_target="Cholesky" | custom-call | tf_op jit(solution)/shard_map/jit(cholesky)/cholesky | solution.py:411
  103.2 0.6 compare_reduce_fusion
  103.8 0.7 fusion.15
  104.5 4.9 %custom-call.6 = f32[1,64,64]{1,2,0:T(8,128)S(1)} custom-call(f32[1,64,64]{2,1,0:T(8,128)S(1)} %fusion.15), custom_call_target="InvertDiagBlocksLowerTriangular" | custom-call | tf_op jit(solution)/shard_map/triangular_solve | solution.py:412
  109.4 0.2 convolution_bitcast_fusion.1
  109.6 2.0 %fusion.3 = f32[64,8,6,128]{3,0,1,2:T(8,128)S(1)} fusion(f32[64,64,1,1]{1,0,3,2:T(8,128)S(1)} %convolution_bitcast_fusion.1, f32[64,6,8,128]{3,2,1,0:T(8,128)S(1)} %bitcast.115), kind=kOutput, calls=%fused_computation.8 | convolution fusion | flops 301989888 | bytes 3162112 | tf_op jit(solution)/shard_map/mn,nxoy->moxy/dot_general | solution.py:415
  111.6 2.1 %copy.11 = f32[64,8,6,128]{3,1,2,0:T(8,128)} copy(f32[64,8,6,128]{3,0,1,2:T(8,128)S(1)} %fusion.3) | data formatting | bytes 3145728 | tf_op jit(solution)/shard_map/mn,nxoy->moxy/transpose | solution.py:415
  (17 shorter events, 0.2 us)
Async XLA Ops:
  0.0 1.0 copy-start
  2.6 1.4 %copy-start.1 = (f32[64,8,6,128]{3,1,2,0:T(8,128)S(1)}, f32[64,8,6,128]{3,1,2,0:T(8,128)}, u32[]{:S(2)}) copy-start(f32[64,8,6,128]{3,1,2,0:T(8,128)} %param.4) | copy-start | bytes 4718596
  2.6 1.4 %copy-start.2 = (f32[8,6,128]{2,0,1:T(8,128)S(1)}, f32[8,6,128]{2,0,1:T(8,128)}, u32[]{:S(2)}) copy-start(f32[8,6,128]{2,0,1:T(8,128)} %param.6) | copy-start | bytes 73732

commit v2 on v1

--- a/solution.py
+++ b/solution.py
@@ -105,26 +105,40 @@
     return high, low
 
 
-def band_weights(stencil):
+def spread_stencil(stencil):
     side = 2 * REACH + 1
     t = jnp.transpose(stencil, (2, 3, 1, 0)).reshape(side * side * ORB, ORB)
     lane = jnp.arange(LANES)
     spread = (lane[None, :] // TY == jnp.arange(ORB)[:, None]).astype(jnp.float32)
-    wide = jnp.dot(t, spread, precision=lax.Precision.HIGHEST, preferred_element_type=jnp.float32)
-    wide = wide.reshape(side, side, 1, ORB, 1, LANES)
-    yy = jnp.arange(TY)
-    rel = jnp.stack([yy, jnp.where(yy < TY // 2, yy + TY, yy - TY)])
-    dy = rel[:, :, None] - (lane % TY)[None, None, :]
-    total = jnp.zeros((side, 2, ORB, TY, LANES), jnp.float32)
-    for k in range(side):
-        total = total + jnp.where((dy == k - REACH)[None, :, None], wide[:, k], 0.0)
-    band = total.reshape(side, 2 * LANES, LANES)
-    zero = jnp.zeros((1, 2 * LANES, LANES), jnp.float32)
-    full = jnp.concatenate(
-        [jnp.concatenate([band, zero], axis=0), jnp.concatenate([zero, band], axis=0)], axis=2
-    )
-    high = lax.reduce_precision(full, 8, 7)
-    return high.astype(jnp.bfloat16), (full - high).astype(jnp.bfloat16)
+    return jnp.dot(t, spread, precision=lax.Precision.HIGHEST, preferred_element_type=jnp.float32)
+
+
+def band_weights(wide_ref, wh_ref, wl_ref):
+    side = 2 * REACH + 1
+    yy = lax.broadcasted_iota(jnp.int32, (TY, LANES), 0)
+    y = lax.rem(lax.broadcasted_iota(jnp.int32, (TY, LANES), 1), TY)
+    empty = jnp.zeros((2 * LANES, LANES), jnp.bfloat16)
+    for ref in (wh_ref, wl_ref):
+        ref[0, :, pl.ds(LANES, LANES)] = empty
+        ref[side, :, pl.ds(0, LANES)] = empty
+
+    def one(dx, carry):
+        for part in range(2):
+            rel = yy if part == 0 else jnp.where(yy < TY // 2, yy + TY, yy - TY)
+            dy = rel - y
+            for p in range(ORB):
+                total = jnp.zeros((TY, LANES), jnp.float32)
+                for k in range(side):
+                    row = wide_ref[dx, k, pl.ds(p, 1), :]
+                    total = jnp.where(dy == k - REACH, row, total)
+                high, low = split_bf16(total)
+                rows = pl.ds(part * LANES + p * TY, TY)
+                for xr in range(2):
+                    wh_ref[dx + xr, rows, pl.ds(xr * LANES, LANES)] = high
+                    wl_ref[dx + xr, rows, pl.ds(xr * LANES, LANES)] = low
+        return carry
+
+    lax.fori_loop(0, side, one, 0)
 
 
 def swap_blocks(value):
@@ -140,9 +154,9 @@
 
 
 def filter_kernel(
-    sizes, block_ref, onsite_ref, wh_ref, wl_ref, out_ref, gram_ref,
-    recv, energies, state, sh, sl, back, gathered, grams,
-    send_sems, recv_sems, local_sems, back_send, back_recv, back_local, gram_send, gram_recv,
+    sizes, block_ref, onsite_ref, wide_ref, out_ref, gram_ref,
+    wh_ref, wl_ref, recv, columns, energies, state, sh, sl, back, gathered, grams, sums,
+    send_sems, recv_sems, local_sems, back_send, back_recv, back_local, small_send, small_recv, out_sem,
 ):
     ngx, ngy, chunks, lx = sizes
     peers = ngx * ngy
@@ -171,15 +185,33 @@
     def landing(c):
         return recv.at[c, gy, pl.ds(gx * piece, piece)]
 
-    def send_onsite(k, carry):
-        pltpu.make_async_remote_copy(
-            src_ref=onsite_ref, dst_ref=landing(chunks), send_sem=send_sems.at[chunks],
-            recv_sem=recv_sems.at[chunks], device_id=peer(k)[1], device_id_type=MESH,
-        ).start()
-        return carry
-
-    pltpu.make_async_copy(onsite_ref, landing(chunks), local_sems.at[chunks]).start()
-    lax.fori_loop(1, peers, send_onsite, 0)
+    plane = 2 * ngy
+    nz = ngx // 2
+    z, col = gx // 2, lax.rem(gx, 2)
+    spot = col * ngy + gy
+
+    def along(k):
+        return {"gx": lax.rem(z + k, nz) * 2 + col, "gy": gy}
+
+    def across(k):
+        other = lax.rem(spot + k, plane)
+        return {"gx": z * 2 + other // ngy, "gy": lax.rem(other, ngy)}
+
+    def share(count, where, ref, sem):
+        def one(k, carry):
+            pltpu.make_async_remote_copy(
+                src_ref=ref, dst_ref=ref, send_sem=small_send.at[sem],
+                recv_sem=small_recv.at[sem], device_id=where(k), device_id_type=MESH,
+            ).start()
+            return carry
+
+        lax.fori_loop(1, count, one, 0)
+
+    def settle(refs, sems, sem):
+        pltpu.make_async_copy(refs, refs, sems.at[sem]).wait()
+
+    columns[spot, pl.ds(z * piece, piece)] = onsite_ref[...]
+    share(nz, along, columns.at[spot, pl.ds(z * piece, piece)], 0)
 
     def send_chunk(c, carry):
         pltpu.make_async_copy(
@@ -197,7 +229,11 @@
 
         return lax.fori_loop(1, peers, one, carry)
 
-    lax.fori_loop(0, chunks, send_chunk, 0)
+    send_chunk(0, 0)
+    settle(columns.at[0, pl.ds(0, (nz - 1) * piece)], small_recv, 0)
+    share(plane, across, columns.at[spot], 1)
+    lax.fori_loop(1, chunks, send_chunk, 0)
+    band_weights(wide_ref, wh_ref, wl_ref)
 
     others = (peers - 1) * piece
 
@@ -216,12 +252,14 @@
                     x = q + i
                     store(x % 2, x // 2, g, tile[i])
 
-    wait_chunk(chunks)
-
-    def store_energy(xr, r, g, tile):
-        energies[xr, r, pl.ds(g * 8, 8), :] = tile - shift_centre
-
-    unpack(chunks, store_energy)
+    settle(columns.at[pl.ds(0, plane - 1)], small_recv, 1)
+    for other in range(plane):
+        for q in range(nz):
+            tile = columns[other, pl.ds(q * piece, piece)].reshape(lx, ORB, LANES)
+            tile = swap_blocks(tile) - shift_centre
+            for i in range(lx):
+                x = (2 * q + other // ngy) * lx + i
+                energies[x % 2, x // 2, pl.ds((other % ngy) * 8, 8), :] = tile[i]
 
     lane = lax.broadcasted_iota(jnp.int32, (1, TY, LANES), 2)
     near = lax.rem(lane, TY) < TY // 2
@@ -323,24 +361,20 @@
     total = lax.fori_loop(0, piece // 2, gram_step, total)
     cross = total[nvec:]
     local = total[:nvec] + cross + cross.T
-    grams[me] = jnp.concatenate([local[: nvec // 2], local[nvec // 2:]], axis=1)
-
-    def send_gram(k, carry):
-        pltpu.make_async_remote_copy(
-            src_ref=grams.at[me], dst_ref=grams.at[me], send_sem=gram_send,
-            recv_sem=gram_recv, device_id=peer(k)[1], device_id_type=MESH,
-        ).start()
-        return carry
-
-    lax.fori_loop(1, peers, send_gram, 0)
-    out_copy = pltpu.make_async_copy(gathered, out_ref, local_sems.at[chunks])
+    grams[spot] = jnp.concatenate([local[: nvec // 2], local[nvec // 2:]], axis=1)
+    share(plane, across, grams.at[spot], 2)
+    out_copy = pltpu.make_async_copy(gathered, out_ref, out_sem)
     out_copy.start()
-    pltpu.make_async_copy(
-        grams.at[pl.ds(0, peers - 1)], grams.at[pl.ds(0, peers - 1)], gram_recv
-    ).wait()
+    settle(grams.at[pl.ds(0, plane - 1)], small_recv, 2)
     total = grams[0]
-    for d in range(1, peers):
+    for d in range(1, plane):
         total = total + grams[d]
+    sums[z] = total
+    share(nz, along, sums.at[z], 3)
+    settle(sums.at[pl.ds(0, nz - 1)], small_recv, 3)
+    total = sums[0]
+    for d in range(1, nz):
+        total = total + sums[d]
     gram_ref[...] = total
 
     def drain(c, carry):
@@ -349,7 +383,7 @@
         ).wait()
         return carry
 
-    lax.fori_loop(0, chunks + 1, drain, 0)
+    lax.fori_loop(0, chunks, drain, 0)
 
     def drain_back(c, carry):
         pltpu.make_async_copy(
@@ -358,10 +392,52 @@
         return carry
 
     lax.fori_loop(0, chunks, drain_back, 0)
-    pltpu.make_async_copy(
-        grams.at[pl.ds(0, peers - 1)], grams.at[pl.ds(0, peers - 1)], gram_send
-    ).wait()
+    settle(columns.at[0, pl.ds(0, (nz - 1) * piece)], small_send, 0)
+    settle(columns.at[pl.ds(0, plane - 1)], small_send, 1)
+    settle(grams.at[pl.ds(0, plane - 1)], small_send, 2)
+    settle(sums.at[pl.ds(0, nz - 1)], small_send, 3)
     out_copy.wait()
+
+
+def basis_kernel(count, rows_ref, gram_ref, out_ref):
+    nvec = gram_ref.shape[0] * 2
+    piece = rows_ref.shape[0] // nvec
+    packed = gram_ref[...] / count
+    gram = jnp.concatenate([packed[:, :nvec], packed[:, nvec:]], axis=0)
+    row = lax.broadcasted_iota(jnp.int32, (nvec, nvec), 0)
+    lane = lax.broadcasted_iota(jnp.int32, (nvec, nvec), 1)
+    work = jnp.concatenate([gram, (row == lane).astype(jnp.float32)], axis=1)
+    full = (nvec, 2 * nvec)
+    row = lax.broadcasted_iota(jnp.int32, full, 0)
+    pivots = jnp.ones(full, jnp.float32)
+    panel = 8
+    for first in range(0, nvec, panel):
+        cols = [
+            jnp.broadcast_to(work[:, first + j:first + j + 1], full) for j in range(panel)
+        ]
+        for j in range(panel):
+            k = first + j
+            pivot = cols[j][k:k + 1]
+            factor = jnp.where(row > k, cols[j] * (1.0 / pivot), 0.0)
+            pivots = jnp.where(row == k, pivot, pivots)
+            work = work - factor * work[k:k + 1]
+            for i in range(j + 1, panel):
+                cols[i] = cols[i] - factor * cols[i][k:k + 1]
+    inverse = (work / jnp.sqrt(pivots))[:, nvec:]
+    high, low = split_bf16(inverse)
+    both = jnp.concatenate([high, low], axis=0)
+
+    def one(q, carry):
+        a = rows_ref[pl.ds(2 * q, nvec, stride=piece), :]
+        b = rows_ref[pl.ds(2 * q + 1, nvec, stride=piece), :]
+        vh, vl = split_bf16(jnp.concatenate([a, b], axis=1))
+        twice = jnp.dot(both, vh, preferred_element_type=jnp.float32)
+        out = twice[:nvec] + (twice[nvec:] + jnp.dot(high, vl, preferred_element_type=jnp.float32))
+        out_ref[pl.ds(2 * q, nvec, stride=piece), :] = out[:, :LANES]
+        out_ref[pl.ds(2 * q + 1, nvec, stride=piece), :] = out[:, LANES:]
+        return carry
+
+    lax.fori_loop(0, piece // 2, one, 0)
 
 
 def per_device_whole(block, hop, onsite, offsets):
@@ -371,7 +447,8 @@
     chunks = nvec // peers
     nx = ngx * lx
     piece = lx * ORB
-    wh, wl = band_weights(build_stencil(hop, offsets))
+    side = 2 * REACH + 1
+    wide = spread_stencil(build_stencil(hop, offsets)).reshape(side, side, ORB, LANES)
     rows = jnp.transpose(block, (0, 2, 1, 3)).reshape(nvec * piece, ly)
     energy_rows = jnp.transpose(onsite, (1, 0, 2)).reshape(piece, ly)
     vmem = pl.BlockSpec(memory_space=pltpu.VMEM)
@@ -382,40 +459,43 @@
             jax.ShapeDtypeStruct((nvec * piece, ly), jnp.float32),
             jax.ShapeDtypeStruct((nvec // 2, LANES), jnp.float32),
         ),
-        in_specs=[vmem, vmem, vmem, vmem],
+        in_specs=[hbm, vmem, vmem],
         out_specs=(hbm, vmem),
         scratch_shapes=[
-            pltpu.VMEM((chunks + 1, ngy, nx * ORB, LANES), jnp.float32),
+            pltpu.VMEM((side + 1, 2 * LANES, 2 * LANES), jnp.bfloat16),
+            pltpu.VMEM((side + 1, 2 * LANES, 2 * LANES), jnp.bfloat16),
+            pltpu.VMEM((chunks, ngy, nx * ORB, LANES), jnp.float32),
+            pltpu.VMEM((2 * ngy, ngx // 2 * piece, LANES), jnp.float32),
             pltpu.VMEM((2, nx // 2, TY, LANES), jnp.float32),
             pltpu.VMEM((2, 2, nx // 2, TY, LANES), jnp.float32),
             pltpu.VMEM((2, nx // 2 + REACH, TY, 2 * LANES), jnp.bfloat16),
             pltpu.VMEM((2, nx // 2 + REACH, TY, 2 * LANES), jnp.bfloat16),
             pltpu.VMEM((chunks, ngy, nx * ORB, LANES), jnp.float32),
             pltpu.VMEM((nvec * piece, LANES), jnp.float32),
-            pltpu.VMEM((peers, nvec // 2, LANES), jnp.float32),
-            pltpu.SemaphoreType.DMA((chunks + 1,)),
-            pltpu.SemaphoreType.DMA((chunks + 1,)),
-            pltpu.SemaphoreType.DMA((chunks + 1,)),
+            pltpu.VMEM((2 * ngy, nvec // 2, LANES), jnp.float32),
+            pltpu.VMEM((ngx // 2, nvec // 2, LANES), jnp.float32),
             pltpu.SemaphoreType.DMA((chunks,)),
             pltpu.SemaphoreType.DMA((chunks,)),
             pltpu.SemaphoreType.DMA((chunks,)),
-            pltpu.SemaphoreType.DMA,
+            pltpu.SemaphoreType.DMA((chunks,)),
+            pltpu.SemaphoreType.DMA((chunks,)),
+            pltpu.SemaphoreType.DMA((chunks,)),
+            pltpu.SemaphoreType.DMA((4,)),
+            pltpu.SemaphoreType.DMA((4,)),
             pltpu.SemaphoreType.DMA,
         ],
         compiler_params=pltpu.CompilerParams(
             collective_id=0, has_side_effects=True, vmem_limit_bytes=48 * 1024 * 1024
         ),
-    )(rows, energy_rows, wh, wl)
-    gram = jnp.concatenate([packed[:, :nvec], packed[:, nvec:]], axis=0)
-    gram = gram / (piece * ly * peers)
-    lower = jnp.linalg.cholesky(gram)
-    inverse = lax.linalg.triangular_solve(
-        lower, jnp.eye(nvec, dtype=jnp.float32), left_side=True, lower=True
-    )
-    return jnp.einsum(
-        "mn,nxoy->moxy", inverse, filtered.reshape(nvec, lx, ORB, ly),
-        precision=lax.Precision.HIGHEST, preferred_element_type=jnp.float32,
-    )
+    )(rows, energy_rows, wide)
+    basis = pl.pallas_call(
+        functools.partial(basis_kernel, piece * ly * peers),
+        out_shape=jax.ShapeDtypeStruct((nvec * piece, ly), jnp.float32),
+        in_specs=[vmem, vmem],
+        out_specs=vmem,
+        compiler_params=pltpu.CompilerParams(vmem_limit_bytes=32 * 1024 * 1024),
+    )(filtered, packed)
+    return jnp.transpose(basis.reshape(nvec, lx, ORB, ly), (0, 2, 1, 3))
 
 
 def per_device(block, hop, onsite, offsets):
@@ -423,7 +503,7 @@
     nvec, orbitals, lx, ly = block.shape
     fits = (
         nvec % (ngx * ngy) == 0 and nvec == 64 and orbitals == ORB and ly == LANES
-        and ngy == 2 and (ngx * lx) % 16 == 0
+        and ngy == 2 and ngx % 2 == 0 and ngx > 2 and (ngx * lx) % 16 == 0 and lx % 2 == 0
     )
     return (per_device_whole if fits else per_device_halo)(block, hop, onsite, offsets)
 

time: 114 us -> 99.2 us (0.87)
  other arithmetic: 14 us -> 0.86 us
  Pallas kernels: 92.9 us -> 97.2 us
  local copies, waits for them, and re-layouts: 3.6 us -> 0.23 us
  matrix products: 2.96 us -> 0.74 us
    another operation x6 -> x0, other arithmetic: 12.1 us -> none  [the longest x3 6.52 us: per_device_whole(): lower = jnp.linalg.cholesky(gram)]
    pallas_call x0 -> x1, Pallas kernels: none -> 8.34 us  [per_device_whole(): pl.pallas_call(functools.partial(basis_kernel, piece * ly * peers), out_s...]
    pallas_call x1, Pallas kernels: 92.9 us -> 88.8 us  [per_device_whole(): pl.pallas_call(functools.partial(filter_kernel, (ngx, ngy, chunks, lx)),...]
    transpose x1 -> x0, local copies, waits for them, and re-layouts: 2.06 us -> none  [per_device_whole(): jnp.einsum('mn,nxoy->moxy', inverse, filtered.reshape(nvec, lx, ORB, ly),...]
    dot_general x2 -> x1, matrix products: 2.29 us -> 0.3 us  [spread_stencil(): jnp.dot(t, spread, precision=lax.Precision.HIGHEST, preferred_element_typ...]
where the time goes in v2:
time: 99.2 us; the launch traced here: 99.1 us
  Pallas kernels  97.2 us (98%)
    pallas_call x1, Pallas kernels, per_device_whole(): pl.pallas_call(functools.partial(filter_kernel, (ngx, ngy, chunks, lx)),...  88.8 us
    pallas_call x1, Pallas kernels, per_device_whole(): pl.pallas_call(functools.partial(basis_kernel, piece * ly * peers), out_s...  8.34 us

profile of v2, /device:TPU:0, one launch (start us, length us, event | category | flops | bytes accessed | tf_op | source)
XLA Modules:
  0.0 99.1 jit_solution(13822196423462675985)
XLA Ops:
  0.0 0.0 copy-start
  0.0 0.0 copy-start.2
  0.0 0.0 copy-start.1
  0.0 0.8 add_bitcast_fusion
  0.8 0.0 copy-done
  0.8 0.4 fusion.4
  1.3 0.1 rev.3
  1.4 0.1 copy.5
  1.6 0.3 fusion.2.wide_ref
  1.9 0.0 copy-done.2
  1.9 0.0 copy-done.1
  1.9 88.8 %shard_map.46 = (f32[3072,128]{1,0:T(8,128)S(1)}, f32[32,128]{1,0:T(8,128)S(1)}) custom-call(f32[3072,128]{1,0:T(8,128)S(1)} %bitcast.39, f32[48,128]{1,0:T(8,128)S(1)} %bitcast.40, f32[7,7,8,128]{3,2,1,0:T(8,128)S(1)} %fusion.2.wide_ref), custom_call_target="tpu_custom_call" | custom-call | tf_op jit(solution)/shard_map/pallas_call | solution.py:456
  90.7 8.3 %shard_map.47 = f32[3072,128]{1,0:T(8,128)} custom-call(f32[3072,128]{1,0:T(8,128)S(1)} %get-tuple-element.7.rows_ref, f32[32,128]{1,0:T(8,128)S(1)} %get-tuple-element.8.gram_ref), custom_call_target="tpu_custom_call" | custom-call | tf_op jit(solution)/shard_map/pallas_call | solution.py:491
  (3 shorter events, 0.0 us)
Async XLA Ops:
  0.0 0.8 copy-start
  0.0 1.9 %copy-start.2 = (f32[8,6,128]{2,0,1:T(8,128)S(1)}, f32[8,6,128]{2,0,1:T(8,128)}, u32[]{:S(2)}) copy-start(f32[8,6,128]{2,0,1:T(8,128)} %param.6) | copy-start | bytes 73732
  0.0 1.9 %copy-start.1 = (f32[64,8,6,128]{3,1,2,0:T(8,128)S(1)}, f32[64,8,6,128]{3,1,2,0:T(8,128)}, u32[]{:S(2)}) copy-start(f32[64,8,6,128]{3,1,2,0:T(8,128)} %param.4) | copy-start | bytes 4718596

commit v3 on v2

--- a/solution.py
+++ b/solution.py
@@ -358,7 +358,7 @@
             preferred_element_type=jnp.float32,
         )
 
-    total = lax.fori_loop(0, piece // 2, gram_step, total)
+    total = lax.fori_loop(0, piece // 2, gram_step, total, unroll=8)
     cross = total[nvec:]
     local = total[:nvec] + cross + cross.T
     grams[spot] = jnp.concatenate([local[: nvec // 2], local[nvec // 2:]], axis=1)
@@ -437,7 +437,7 @@
         out_ref[pl.ds(2 * q + 1, nvec, stride=piece), :] = out[:, LANES:]
         return carry
 
-    lax.fori_loop(0, piece // 2, one, 0)
+    lax.fori_loop(0, piece // 2, one, 0, unroll=4)
 
 
 def per_device_whole(block, hop, onsite, offsets):

time: 99.2 us -> 92.8 us (0.935)
  Pallas kernels: 97.2 us -> 90.8 us
    pallas_call x1, Pallas kernels: 8.34 us -> 4.93 us  [per_device_whole(): pl.pallas_call(functools.partial(basis_kernel, piece * ly * peers), out_s...]
    pallas_call x1, Pallas kernels: 88.8 us -> 85.9 us  [per_device_whole(): pl.pallas_call(functools.partial(filter_kernel, (ngx, ngy, chunks, lx)),...]
where the time goes in v3:
time: 92.8 us; the launch traced here: 92.7 us
  Pallas kernels  90.8 us (98%)
    pallas_call x1, Pallas kernels, per_device_whole(): pl.pallas_call(functools.partial(filter_kernel, (ngx, ngy, chunks, lx)),...  85.9 us
    pallas_call x1, Pallas kernels, per_device_whole(): pl.pallas_call(functools.partial(basis_kernel, piece * ly * peers), out_s...  4.93 us

profile of v3, /device:TPU:0, one launch (start us, length us, event | category | flops | bytes accessed | tf_op | source)
XLA Modules:
  0.0 92.7 jit_solution(7004738132721835835)
XLA Ops:
  0.0 0.0 copy-start
  0.0 0.0 copy-start.2
  0.0 0.0 copy-start.1
  0.0 0.8 add_bitcast_fusion
  0.8 0.0 copy-done
  0.8 0.4 fusion.4
  1.3 0.1 rev.3
  1.4 0.1 copy.5
  1.6 0.3 fusion.2.wide_ref
  1.9 0.0 copy-done.2
  1.9 0.0 copy-done.1
  1.9 85.9 %shard_map.46 = (f32[3072,128]{1,0:T(8,128)S(1)}, f32[32,128]{1,0:T(8,128)S(1)}) custom-call(f32[3072,128]{1,0:T(8,128)S(1)} %bitcast.39, f32[48,128]{1,0:T(8,128)S(1)} %bitcast.40, f32[7,7,8,128]{3,2,1,0:T(8,128)S(1)} %fusion.2.wide_ref), custom_call_target="tpu_custom_call" | custom-call | tf_op jit(solution)/shard_map/pallas_call | solution.py:456
  87.8 4.9 %shard_map.47 = f32[3072,128]{1,0:T(8,128)} custom-call(f32[3072,128]{1,0:T(8,128)S(1)} %get-tuple-element.7.rows_ref, f32[32,128]{1,0:T(8,128)S(1)} %get-tuple-element.8.gram_ref), custom_call_target="tpu_custom_call" | custom-call | tf_op jit(solution)/shard_map/pallas_call | solution.py:491
  (3 shorter events, 0.0 us)
Async XLA Ops:
  0.0 0.8 copy-start
  0.0 1.9 %copy-start.2 = (f32[8,6,128]{2,0,1:T(8,128)S(1)}, f32[8,6,128]{2,0,1:T(8,128)}, u32[]{:S(2)}) copy-start(f32[8,6,128]{2,0,1:T(8,128)} %param.6) | copy-start | bytes 73732
  0.0 1.9 %copy-start.1 = (f32[64,8,6,128]{3,1,2,0:T(8,128)S(1)}, f32[64,8,6,128]{3,1,2,0:T(8,128)}, u32[]{:S(2)}) copy-start(f32[64,8,6,128]{3,1,2,0:T(8,128)} %param.4) | copy-start | bytes 4718596
